TPU v7x, 512 devices: a whole 4x8x8 slice. The times are simulated.
512 devices in a mesh: lat: 64 (over z, y), chan: 8 (over x, core).
Axes of the slice: x: 4, y: 8, z: 8, core: 2. Of those that a mesh axis runs over, the one named last changes fastest.
Arguments:
- field: float32 [256, 1105920], P('chan', 'lat'), may hold values from -6 to 6
- mixing: float32 [128, 2, 256, 256], P('lat', None, 'chan'), may hold values from -6 to 6
Outputs:
- result: float32 [256, 1105920], P('chan', 'lat')
All inputs are finite; a program needn't handle non-finite values.
Results may differ from a plain program's by a relative error of at most 0.0003.
Values sent between devices are 32-bit elements; how exact they have to be, the bound alone decides.
A program may use at most 64 MiB of HBM per device.

v0:
```python
import jax
import jax.numpy as jnp
from jax import lax
from jax.sharding import PartitionSpec as P

NLON = 1440
L = 121
MODES = 128


def legendre(cosv, sinv, mvals):
    log_diag = 0.5 * (
        jnp.log(0.5)
        + lax.lgamma(mvals + 1.5)
        - lax.lgamma(jnp.ones_like(mvals) * 1.5)
        - lax.lgamma(mvals + 1.0)
    )
    pmm = jnp.exp(log_diag[None, :] + mvals[None, :] * jnp.log(sinv)[:, None])
    xcol = cosv[:, None]
    mrow = mvals[None, :]

    def advance(carry, degree):
        prev_one, prev_two = carry
        denom_a = jnp.maximum(degree * degree - mrow * mrow, 1.0)
        coef_a = jnp.sqrt((4.0 * degree * degree - 1.0) / denom_a)
        low = degree - 1.0
        coef_b = jnp.sqrt(
            jnp.maximum(low * low - mrow * mrow, 0.0) / jnp.maximum(4.0 * low * low - 1.0, 1.0)
        )
        general = coef_a * (xcol * prev_one - coef_b * prev_two)
        first = jnp.sqrt(2.0 * mrow + 3.0) * xcol * prev_one
        value = jnp.where(
            degree < mrow,
            0.0,
            jnp.where(degree == mrow, pmm, jnp.where(degree == mrow + 1.0, first, general)),
        )
        return ((value, prev_one), value)

    zeros = jnp.zeros_like(pmm)
    degrees = jnp.arange(L).astype(jnp.float32)
    _, stacked = lax.scan(advance, (zeros, zeros), degrees)
    return jnp.transpose(stacked, (1, 2, 0))


def dft_tables():
    modes = jnp.arange(MODES)
    points = jnp.arange(NLON)
    phase = modes[:, None] * points[None, :] % NLON
    angle = 2.0 * jnp.pi / NLON * phase.astype(jnp.float32)
    return (jnp.cos(angle), jnp.sin(angle))


def colatitudes(rows, total_rows):
    theta = jnp.pi * (rows.astype(jnp.float32) + 0.5) / total_rows
    return (jnp.cos(theta), jnp.sin(theta), jnp.pi / total_rows * jnp.sin(theta))


def channel_mix(coeffs, mixing):
    high = lax.Precision.HIGHEST
    full = lax.all_gather(coeffs, "chan", axis=3, tiled=True)
    mix_re = mixing[:, 0]
    mix_im = mixing[:, 1]
    new_re = jnp.einsum("mlc,mdc->mld", full[:, :, 0], mix_re, precision=high) - jnp.einsum(
        "mlc,mdc->mld", full[:, :, 1], mix_im, precision=high
    )
    new_im = jnp.einsum("mlc,mdc->mld", full[:, :, 0], mix_im, precision=high) + jnp.einsum(
        "mlc,mdc->mld", full[:, :, 1], mix_re, precision=high
    )
    return jnp.stack([new_re, new_im], axis=2)


def shards(field, mixing):
    high = lax.Precision.HIGHEST
    local_chan = field.shape[0]
    band_rows = field.shape[1] // NLON
    bands = lax.axis_size("lat")
    total_rows = band_rows * bands
    band = lax.axis_index("lat")
    cos_tab, sin_tab = dft_tables()
    grid_in = field.reshape(local_chan, band_rows, NLON)
    real_part = jnp.einsum("crn,mn->rmc", grid_in, cos_tab, precision=high) / NLON
    imag_part = -jnp.einsum("crn,mn->rmc", grid_in, sin_tab, precision=high) / NLON
    spec = jnp.stack([real_part, imag_part], axis=2)
    rows = band * band_rows + jnp.arange(band_rows)
    cosv, sinv, weights = colatitudes(rows, total_rows)
    table = legendre(cosv, sinv, jnp.arange(MODES).astype(jnp.float32))
    weighted = table * weights[:, None, None]
    table_part = weighted
    coeffs = lax.psum_scatter(
        jnp.einsum("rml,rmtc->mltc", table_part, spec, precision=high),
        "lat",
        scatter_dimension=0,
        tiled=True,
    )
    mixed = channel_mix(coeffs, mixing)
    table_part = table
    back = jnp.einsum(
        "rml,mltc->rmtc",
        table_part,
        lax.all_gather(mixed, "lat", axis=0, tiled=True),
        precision=high,
    )
    factor = jnp.where(jnp.arange(MODES) == 0, 1.0, 2.0).astype(jnp.float32)
    grid = jnp.einsum(
        "rmc,mn->crn", back[:, :, 0] * factor[None, :, None], cos_tab, precision=high
    ) - jnp.einsum("rmc,mn->crn", back[:, :, 1] * factor[None, :, None], sin_tab, precision=high)
    return jax.nn.gelu(grid, approximate=False).reshape(local_chan, band_rows * NLON)


def solution(mesh):
    placed = (P("chan", "lat"), P("lat", None, "chan", None))
    return jax.shard_map(
        shards, mesh=mesh, in_specs=placed, out_specs=P("chan", "lat"), check_vma=False
    )
```

profile of v0, /device:TPU:1, one launch (start us, length us, event | category | flops | bytes accessed | tf_op | source)
XLA Modules:
  0.0 1067.7 jit_solution(9507855022692257016)
XLA Ops:
  6.6 4.4 reshape.263
  11.0 7.2 fusion.54
  18.2 7.2 fusion.60
  25.5 633.2 %while.19 = (s32[]{:T(128)}, f32[12,128]{1,0:T(8,128)S(1)}, f32[12,128]{1,0:T(8,128)S(1)}, f32[121,12,128]{2,1,0:T(8,128)S(1)}, f32[121]{0:T(128)S(1)}, /*index=...) while((s32[]{:T(128)}, f32[12,128]{1,0:T(8,128)S(1)}, ...), condition=%wide.region_1.2_spmd.clone.clone, body=%wide.region_0.1_spmd.clone.clone.sunk | while | flops 20669 | bytes 48355 | solution.py:41
  25.5 0.7 dynamic_slice.11
  30.8 0.7 dynamic_slice.11
  36.0 0.7 dynamic_slice.11
  41.2 0.7 dynamic_slice.11
  46.5 0.7 dynamic_slice.11
  51.7 0.7 dynamic_slice.11
  56.9 0.7 dynamic_slice.11
  62.1 0.7 dynamic_slice.11
  67.4 0.7 dynamic_slice.11
  72.6 0.7 dynamic_slice.11
  77.8 0.7 dynamic_slice.11
  83.1 0.7 dynamic_slice.11
  658.8 1.2 copy.34
  660.0 1.8 copy.38
  661.9 1.3 fusion.69
  663.1 8.5 fusion.67
  671.7 247.9 %reduce-scatter.2.cloned.1.call-done = f32[2,121,2,32]{1,3,2,0:T(8,128)} async-done(((f32[128,121,2,32]{1,3,2,0:T(8,128)}), f32[2,121,2,32]{1,3,2,0:T(8,128)}) %reduce-scatter.2.cloned.1.call-update) | async-done | bytes 61968 | tf_op jit(solution)/shard_map/reduce_scatter | solution.py:89
  919.6 18.9 %all_gather.6 = f32[2,121,2,256]{1,3,2,0:T(8,128)S(1)} all-gather(f32[2,121,2,32]{1,3,2,0:T(8,128)} %reduce-scatter.2.cloned.1.call-done), channel_id=1, replica_groups=mesh['lat'=64,'chan'=8] {'chan'}, dimensions={3}, use_global_device_ids=true | all-gather | bytes 557568 | tf_op jit(solution)/shard_map/all_gather | solution.py:60
  940.3 0.7 copy.56
  941.0 78.7 %all-gather.2.cloned.1.call-done = f32[128,121,2,32]{1,3,0,2:T(8,128)} async-done(((f32[2,121,2,32]{1,3,0,2:T(8,128)}), f32[128,121,2,32]{1,3,0,2:T(8,128)}) %all-gather.2.cloned.1.call-update) | async-done | bytes 3964944 | tf_op jit(solution)/shard_map/all_gather | solution.py:100
  1019.6 18.2 %fusion.45 = f32[12,128,2,32]{3,0,2,1:T(8,128)S(1)} fusion(f32[12,128,121,1]{2,0,3,1:T(8,128)S(1)} %copy.56, f32[128,121,2,32]{1,3,0,2:T(8,128)} %all-gather.2.cloned.1.call-done), kind=kOutput, calls=%fused_computation.57 | convolution fusion | flops 142737408 | bytes 5101568 | tf_op jit(solution)/shard_map/rml,mltc->rmtc/dot_general | solution.py:97
  1038.0 1.0 copy.48
  1039.1 5.8 fusion.78
  1044.8 1.0 copy.49
  1045.8 5.8 fusion.81
  1051.6 5.3 fusion.25
  1057.0 1.4 copy.50
  1058.4 2.2 reshape.264
  (856 shorter events, 244.9 us)
Async XLA Ops:
  6.5 913.1 %reduce-scatter.2.cloned.1.call-start = ((), (), s32[]{:S(2)}) async-start(), calls=%async_computation.1 | async-start | bytes 4259840 | tf_op jit(solution)/shard_map/reduce_scatter | solution.py:89
  671.6 266.9 %copy-start = (f32[2,2,32,256]{3,2,1,0:T(8,128)S(1)}, f32[2,2,32,256]{3,2,1,0:T(8,128)}, u32[]{:S(2)}) copy-start(f32[2,2,32,256]{3,2,1,0:T(8,128)} %param.5) | copy-start | bytes 393220
  671.6 348.0 %all-gather.2.cloned.1.call-start = ((), (), s32[]{:S(2)}) async-start(), calls=%async_computation.2 | async-start | bytes 4259840 | tf_op jit(solution)/shard_map/all_gather | solution.py:100
Sparse Core Ops, SparseCore 0:
  671.8 247.8 reduce-scatter.1
  940.4 79.2 all-gather.1
where the time goes:
time: 1090 us; the launch traced here: 1070 us
  loops' own time  383 us (35%)
  waiting for transfers between devices  327 us (30%)
  other arithmetic  180 us (17%)
  local copies, waits for them, and re-layouts  92.4 us (8%)
  matrix products  53.8 us (5%)
  blocking collectives  18.9 us (2%)
  between operations  13.8 us (1%)
    another operation x1, loops' own time, legendre(): _, stacked = lax.scan(advance, (zeros, zeros), degrees)  383 us
    reduce_scatter x1, waiting for transfers between devices, shards(): lax.psum_scatter(jnp.einsum('rml,rmtc->mltc', table_part, spec, precision...  248 us
    all_gather x1, waiting for transfers between devices, shards(): lax.all_gather(mixed, 'lat', axis=0, tiled=True)  78.7 us
    dynamic_slice x121, local copies, waits for them, and re-layouts, legendre(): _, stacked = lax.scan(advance, (zeros, zeros), degrees)  78.7 us
    eq x121, other arithmetic, advance(): degree == mrow + 1.0  76.3 us
    lt x121, other arithmetic, advance(): degree < mrow  75.9 us
  transfers between devices with their start and end apart: 2, of which 2 were waited for; matrix products, arithmetic and copies ran while one was open for 0% of the time, Pallas kernels for 0%

commit v1 on v0

v1 whole, which is shorter than its diff:
```python
import functools

import jax
import jax.numpy as jnp
import ml_dtypes
import numpy as np
from jax import lax
from jax.experimental import pallas as pl
from jax.experimental.pallas import tpu as pltpu
from jax.sharding import PartitionSpec as P
from math import lgamma

NLON = 1440
L = 121
MODES = 128
NLAT = 768
BANDS = 64
CHANS = 8
WIN = 1536
GROUP = 4
GROUPS = 3
SPAN = GROUP * NLON
MESH = pl.DeviceIdType.MESH
F32 = jnp.float32
BF16 = jnp.bfloat16


def split(table):
    high = table.astype(np.float32).astype(ml_dtypes.bfloat16)
    low = (table - high.astype(np.float64)).astype(ml_dtypes.bfloat16)
    return high, low


def dft_tables():
    n = np.arange(NLON)
    col = np.arange(2 * MODES)
    quarter, k = col // 64, col % 64
    m = 2 * k + quarter // 2
    angle = 2.0 * np.pi / NLON * ((n[:, None] * m[None, :]) % NLON)
    wave = np.where(quarter[None, :] % 2 == 0, np.cos(angle), -np.sin(angle))
    forward = np.zeros((WIN, 2 * MODES))
    forward[:NLON] = wave / NLON
    backward = np.zeros((2 * MODES, WIN))
    backward[:, :NLON] = (wave * np.where(m == 0, 1.0, 2.0)[None, :]).T
    return split(forward), split(backward)


def row_constants():
    j = np.arange(NLAT)
    place = j // 256, j % 256 // GROUP, j % GROUP
    row = 12 * place[1] + GROUP * place[0] + place[2]
    theta = np.pi * (row + 0.5) / NLAT
    out = np.zeros((8, NLAT))
    out[0] = np.cos(theta)
    out[1] = np.log(np.sin(theta))
    out[2] = np.pi / NLAT * np.sin(theta)
    diag = [
        0.5 * (np.log(0.5) + lgamma(m + 1.5) - lgamma(1.5) - lgamma(m + 1.0)) for m in range(MODES)
    ]
    return out.astype(np.float32), np.repeat(np.array(diag)[:, None], 128, 1).astype(np.float32)


def halves(value):
    high = value.astype(BF16)
    return high, (value - high.astype(F32)).astype(BF16)


def dot(a, b):
    return jnp.dot(a, b, preferred_element_type=F32)


def lane_mask(rows):
    return lax.broadcasted_iota(jnp.int32, (rows, 128), 1) < 64


def forward_rows(block, fh, fl):
    rows = []
    for s in range(GROUP):
        window = block[:, 1408 * s : 1408 * s + WIN]
        rows.append(window if s == 0 else pltpu.roll(window, WIN - 32 * s, 1))
    high, low = halves(jnp.concatenate(rows, 0))
    both = dot(jnp.concatenate([high, low], 0), fh)
    z = both[:128] + both[128:] + dot(high, fl)
    lt = lane_mask(32)
    out = []
    for p in range(2):
        pieces = []
        for half in range(2):
            z0 = z[64 * p : 64 * p + 32, 128 * half : 128 * half + 128]
            z1 = z[64 * p + 32 : 64 * p + 64, 128 * half : 128 * half + 128]
            pieces.append(jnp.where(lt, z0, pltpu.roll(z1, 64, 1)))
            pieces.append(jnp.where(lt, pltpu.roll(z0, 64, 1), z1))
        v = jnp.concatenate(pieces, 0).T
        out += [v[:64], v[64:]]
    return out


def backward_lhs(quarters):
    lt = lane_mask(32)
    rows = []
    for p in range(2):
        u = jnp.concatenate([quarters[2 * p], quarters[2 * p + 1]], 0).T
        u0, u1, u2, u3 = (u[32 * q : 32 * q + 32] for q in range(4))
        rows.append(
            jnp.concatenate(
                [jnp.where(lt, u0, pltpu.roll(u1, 64, 1)), jnp.where(lt, u2, pltpu.roll(u3, 64, 1))], 1
            )
        )
        rows.append(
            jnp.concatenate(
                [jnp.where(lt, pltpu.roll(u0, 64, 1), u1), jnp.where(lt, pltpu.roll(u2, 64, 1), u3)], 1
            )
        )
    return jnp.concatenate(rows, 0)


def gelu(v):
    return 0.5 * v * (1.0 + lax.erf(v * np.float32(np.sqrt(0.5))))


def legendre_tables(me, rowc, ldt, coef, table, pw, pt):
    for mh in range(2):
        m = 2 * me + mh
        mf = m.astype(F32)
        deg = lax.broadcasted_iota(jnp.int32, (128, 128), 0).astype(F32)
        denom = jnp.maximum(deg * deg - mf * mf, 1.0)
        ca = jnp.sqrt(jnp.maximum(4.0 * deg * deg - 1.0, 0.0) / denom)
        low = deg - 1.0
        cb = jnp.sqrt(jnp.maximum(low * low - mf * mf, 0.0) / jnp.maximum(4.0 * low * low - 1.0, 1.0))
        first = jnp.sqrt(2.0 * mf + 3.0 + jnp.zeros_like(deg))
        coef[3 * mh] = jnp.where(deg > mf + 1.0, ca, jnp.where(deg == mf + 1.0, first, 0.0))
        coef[3 * mh + 1] = jnp.where(deg > mf + 1.0, ca * cb, 0.0)
        coef[3 * mh + 2] = jnp.where(deg == mf, 1.0, 0.0)
    xcol = rowc[0:1, :]
    logsin = rowc[1:2, :]
    wide = lambda ref, mh, l: jnp.concatenate([ref[mh, pl.ds(l, 1), :]] * 6, 1)
    pmm = []
    for mh in range(2):
        m = 2 * me + mh
        diag = jnp.concatenate([ldt[pl.ds(m, 1), :]] * 6, 1)
        pmm.append(jnp.exp(diag + m.astype(F32) * logsin))

    def advance(l, carry):
        out = []
        for mh in range(2):
            one, two = carry[2 * mh], carry[2 * mh + 1]
            value = (
                wide(coef, 3 * mh, l) * xcol * one
                - wide(coef, 3 * mh + 1, l) * two
                + wide(coef, 3 * mh + 2, l) * pmm[mh]
            )
            table[pl.ds(128 * mh + l, 1), :] = value
            out += [value, one]
        return tuple(out)

    zero = xcol * 0.0
    for mh in range(2):
        table[128 * mh + 120 : 128 * mh + 128, :] = jnp.zeros((8, NLAT), F32)
    lax.fori_loop(0, L, advance, (zero,) * 4)

    def lay(g, _):
        part = table[:, pl.ds(pl.multiple_of(256 * g, 256), 256)]
        weight = rowc[2:3, pl.ds(pl.multiple_of(256 * g, 256), 256)]
        high, low = halves(part * weight)
        pw[0, g], pw[1, g] = high, low
        high, low = halves(part.T)
        pt[0, g], pt[1, g] = high, low
        return 0

    lax.fori_loop(0, GROUPS, lay, 0)


def mixing_tables(mixv, wm):
    group = lax.broadcasted_iota(jnp.int32, (32, 128), 1) // 32
    for src in range(CHANS):
        at, g = src // 4, src % 4
        pieces = []
        for mh in range(2):
            re = mixv[mh, 0][:, 128 * at : 128 * at + 128]
            im = mixv[mh, 1][:, 128 * at : 128 * at + 128]
            for a, b in ((re, -im), (im, re)):
                put = lambda v, to: jnp.where(
                    group == to, v if to == g else pltpu.roll(v, 32 * ((to - g) % 4), 1), 0.0
                )
                pieces.append(put(a, 2 * mh) + put(b, 2 * mh + 1))
        high, low = halves(jnp.concatenate(pieces, 0).T)
        wm[128 * src : 128 * src + 128, :] = jnp.concatenate([high, low], 1)


def kernel(
    x_hbm, mix_hbm, fh_hbm, fl_hbm, ih_hbm, il_hbm, rowc, ldt, out_hbm,
    xv, fv, iv, mixv, sent, got, back, home, gath, coef, table, pw, pt, wm, ybuf, yv,
    xsem, fsem, isem, msem, osem, send1, recv1, send2, recv2, gsend, grecv,
):
    me = lax.axis_index("lat")
    ch = lax.axis_index("chan")

    def x_copy(g):
        return pltpu.make_async_copy(
            x_hbm.at[:, pl.ds(pl.multiple_of(SPAN * g, 128), SPAN)], xv.at[g], xsem.at[g]
        )

    def out_copy(g):
        return pltpu.make_async_copy(
            yv.at[g], out_hbm.at[:, pl.ds(pl.multiple_of(SPAN * g, 128), SPAN)], osem.at[g]
        )

    f_copies = [
        pltpu.make_async_copy(h, fv.at[i], fsem.at[i]) for i, h in enumerate((fh_hbm, fl_hbm))
    ]
    i_copies = [
        pltpu.make_async_copy(h, iv.at[i], isem.at[i]) for i, h in enumerate((ih_hbm, il_hbm))
    ]
    m_copy = pltpu.make_async_copy(mix_hbm, mixv, msem)
    f_copies[0].start()
    f_copies[1].start()
    for g in range(GROUPS):
        x_copy(g).start()
    m_copy.start()
    i_copies[0].start()
    i_copies[1].start()

    barrier = pltpu.get_barrier_semaphore()

    def greet_lat(i, _):
        pl.semaphore_signal(
            barrier, inc=1, device_id=(lax.rem(me + i, BANDS), ch), device_id_type=MESH
        )
        return 0

    def greet_chan(i, _):
        pl.semaphore_signal(
            barrier, inc=1, device_id=(me, lax.rem(ch + i, CHANS)), device_id_type=MESH
        )
        return 0

    lax.fori_loop(1, BANDS, greet_lat, 0)
    lax.fori_loop(1, CHANS, greet_chan, 0)
    pl.semaphore_wait(barrier, BANDS - 1 + CHANS - 1)

    def spread(src, dst, send, recv, g):
        def one(i, _):
            peer = lax.rem(me + i, BANDS)
            pltpu.make_async_remote_copy(
                src_ref=src.at[g, pl.ds(pl.multiple_of(4 * peer, 4), 4)],
                dst_ref=dst.at[g, pl.ds(pl.multiple_of(4 * me, 4), 4)],
                send_sem=send.at[g],
                recv_sem=recv.at[g],
                device_id=(peer, ch),
                device_id_type=MESH,
            ).start()
            return 0

        lax.fori_loop(1, BANDS, one, 0)
        own = pl.ds(pl.multiple_of(4 * me, 4), 4)
        pltpu.make_async_copy(src.at[g, own], dst.at[g, own], recv.at[g]).start()

    def arrived(dst, recv, g):
        pltpu.make_async_copy(dst.at[g], dst.at[g], recv.at[g]).wait()

    def gone(src, send, g):
        most = pl.ds(0, 4 * (BANDS - 1))
        pltpu.make_async_copy(src.at[g, most], src.at[g, most], send.at[g]).wait()

    f_copies[0].wait()
    f_copies[1].wait()

    def dft(g, _):
        x_copy(g).wait()
        parts = forward_rows(xv[g], fv[0], fv[1])
        for s in range(GROUP):
            sent[g, pl.ds(s, BANDS, stride=GROUP), :] = parts[s]
        spread(sent, got, send1, recv1, g)
        return 0

    lax.fori_loop(0, GROUPS, dft, 0)

    legendre_tables(me, rowc, ldt, coef, table, pw, pt)
    m_copy.wait()
    mixing_tables(mixv, wm)

    total = jnp.zeros((256, 128), F32)
    for g in range(GROUPS):
        arrived(got, recv1, g)
        high, low = halves(got[g])
        both = dot(pw[0, g], jnp.concatenate([high, low], 1))
        total = total + both[:, :128] + both[:, 128:] + dot(pw[1, g], high)
    lt = lane_mask(128)
    gath[ch] = jnp.where(lt, total[:128], total[128:])

    def gather(i):
        return pltpu.make_async_remote_copy(
            src_ref=gath.at[ch],
            dst_ref=gath.at[ch],
            send_sem=gsend.at[i],
            recv_sem=grecv.at[i],
            device_id=(me, lax.rem(ch + i, CHANS)),
            device_id_type=MESH,
        )

    for i in range(1, CHANS):
        gather(i).start()
    for i in range(1, CHANS):
        gather(i).wait()
    high, low = halves(jnp.concatenate([gath[src] for src in range(CHANS)], 1))
    both = dot(high, wm[...])
    mixed = both[:, :128] + both[:, 128:] + dot(low, wm[:, :128])

    stacked = jnp.concatenate([jnp.where(lt, mixed, 0.0), jnp.where(lt, 0.0, mixed)], 0)
    mhigh, mlow = halves(stacked)
    mboth = jnp.concatenate([mhigh, mlow], 1)
    for g in range(GROUPS):
        both = dot(pt[0, g], mboth)
        back[g] = both[:, :128] + both[:, 128:] + dot(pt[1, g], mhigh)
        spread(back, home, send2, recv2, g)
    i_copies[0].wait()
    i_copies[1].wait()

    def inverse(g, _):
        arrived(home, recv2, g)
        z = backward_lhs([home[g, pl.ds(s, BANDS, stride=GROUP), :] for s in range(GROUP)])
        high, low = halves(z)
        stack = jnp.concatenate([high, low], 0)
        for t in range(WIN // 256):
            cols = slice(256 * t, 256 * t + 256)
            both = dot(stack, iv[0, :, cols])
            ybuf[:, cols] = both[:128] + both[128:] + dot(high, iv[1, :, cols])
        last = None
        lane = lax.broadcasted_iota(jnp.int32, (32, 128), 1)
        for s in range(GROUP):
            row = ybuf[32 * s : 32 * s + 32, :]
            at = 1408 * s
            first = row[:, :128]
            if s > 0:
                row = pltpu.roll(row, 32 * s, 1)
                first = jnp.where(lane < 32 * s, last, row[:, :128])
            last = row[:, 1408:]
            yv[g, :, at : at + 128] = gelu(first)
            yv[g, :, at + 128 : at + 1408] = gelu(row[:, 128:1408])
        yv[g, :, SPAN - 128 :] = gelu(last)
        out_copy(g).start()
        return 0

    lax.fori_loop(0, GROUPS, inverse, 0)
    for g in range(GROUPS):
        gone(sent, send1, g)
        gone(back, send2, g)
        out_copy(g).wait()


def shards(field, mixing):
    (fh, fl), (ih, il) = dft_tables()
    rowc, ldt = row_constants()
    anywhere = pl.BlockSpec(memory_space=pl.ANY)
    inside = pl.BlockSpec(memory_space=pltpu.VMEM)
    dma = pltpu.SemaphoreType.DMA
    exchange = pltpu.VMEM((GROUPS, 4 * BANDS, 128), F32)
    return pl.pallas_call(
        kernel,
        out_shape=jax.ShapeDtypeStruct(field.shape, F32),
        in_specs=[anywhere] * 6 + [inside] * 2,
        out_specs=anywhere,
        scratch_shapes=[
            pltpu.VMEM((GROUPS, 32, SPAN), F32),
            pltpu.VMEM((2, WIN, 256), BF16),
            pltpu.VMEM((2, 256, WIN), BF16),
            pltpu.VMEM((2, 2, 32, 256), F32),
            exchange,
            exchange,
            exchange,
            exchange,
            pltpu.VMEM((CHANS, 128, 128), F32),
            pltpu.VMEM((6, 128, 128), F32),
            pltpu.VMEM((256, NLAT), F32),
            pltpu.VMEM((2, GROUPS, 256, 256), BF16),
            pltpu.VMEM((2, GROUPS, 256, 256), BF16),
            pltpu.VMEM((128 * CHANS, 256), BF16),
            pltpu.VMEM((128, WIN), F32),
            pltpu.VMEM((GROUPS, 32, SPAN), F32),
            dma((GROUPS,)),
            dma((2,)),
            dma((2,)),
            dma,
            dma((GROUPS,)),
            dma((GROUPS,)),
            dma((GROUPS,)),
            dma((GROUPS,)),
            dma((GROUPS,)),
            dma((CHANS,)),
            dma((CHANS,)),
        ],
        compiler_params=pltpu.CompilerParams(
            collective_id=0, has_side_effects=True, vmem_limit_bytes=40 << 20
        ),
        cost_estimate=pl.CostEstimate(flops=2_000_000_000, bytes_accessed=8_000_000, transcendentals=600_000),
    )(
        field,
        mixing,
        jnp.asarray(fh),
        jnp.asarray(fl),
        jnp.asarray(ih),
        jnp.asarray(il),
        jnp.asarray(rowc),
        jnp.asarray(ldt),
    )


def solution(mesh):
    placed = (P("chan", "lat"), P("lat", None, "chan", None))
    return jax.shard_map(
        shards, mesh=mesh, in_specs=placed, out_specs=P("chan", "lat"), check_vma=False
    )
```

time: 1090 us -> 64.1 us (0.06); the launches traced: 1070 us -> 63.6 us
  loops' own time: 383 us -> 0 us
  waiting for transfers between devices: 327 us -> 0 us
  other arithmetic: 180 us -> 0 us
  local copies, waits for them, and re-layouts: 92.4 us -> 9.99 us
  matrix products: 53.8 us -> 0 us
  Pallas kernels: 0 us -> 53.6 us
  blocking collectives: 18.9 us -> 0 us
  between operations: 13.8 us -> 0.02 us
    another operation x1 -> x0, loops' own time: 383 us -> none  [legendre(): _, stacked = lax.scan(advance, (zeros, zeros), degrees)]
    reduce_scatter x1 -> x0, waiting for transfers between devices: 248 us -> none  [shards(): lax.psum_scatter(jnp.einsum('rml,rmtc->mltc', table_part, spec, precision...]
    all_gather x1 -> x0, waiting for transfers between devices: 78.7 us -> none  [shards(): lax.all_gather(mixed, 'lat', axis=0, tiled=True)]
    dynamic_slice x121 -> x0, local copies, waits for them, and re-layouts: 78.7 us -> none  [legendre(): _, stacked = lax.scan(advance, (zeros, zeros), degrees)]
    eq x121 -> x0, other arithmetic: 76.3 us -> none  [advance(): degree == mrow + 1.0]
    lt x121 -> x0, other arithmetic: 75.9 us -> none  [advance(): degree < mrow]
    pallas_call x0 -> x1, Pallas kernels: none -> 53.6 us  [shards(): pl.pallas_call(kernel, out_shape=jax.ShapeDtypeStruct(field.shape, F32),...]
    dot_general x8 -> x0, matrix products: 42.2 us -> none  [the longest x1 18.2 us: shards(): jnp.einsum('rml,mltc->rmtc', table_part, lax.all_gather(mixed, 'lat', axi...]
  transfers between devices with their start and end apart: 2 -> 0, of which waited for: 2 -> 0; matrix products, arithmetic and copies ran while one was open for 0% -> 0% of each run, Pallas kernels for 0% -> 0%
where the time goes in v1:
time: 64.1 us; the launch traced here: 63.6 us
  Pallas kernels  53.6 us (84%)
  local copies, waits for them, and re-layouts  9.99 us (16%)
    pallas_call x1, Pallas kernels, shards(): pl.pallas_call(kernel, out_shape=jax.ShapeDtypeStruct(field.shape, F32),...  53.6 us
    unnamed x17, local copies, waits for them, and re-layouts  9.99 us

profile of v1, /device:TPU:1, one launch (start us, length us, event | category | flops | bytes accessed | tf_op | source)
XLA Modules:
  0.0 63.6 jit_solution(1838639398359368176)
XLA Ops:
  0.0 0.0 copy-start
  0.0 1.6 %copy-done = f32[32,17280]{1,0:T(8,128)S(1)} copy-done((f32[32,17280]{1,0:T(8,128)S(1)}, f32[32,17280]{1,0:T(8,128)}, u32[]{:S(2)}) %copy-start) | copy-done | bytes 2211864
  1.6 0.0 copy-start.1
  1.6 1.1 %copy-done.1 = bf16[256,1536]{1,0:T(8,128)(2,1)S(1)} copy-done((bf16[256,1536]{1,0:T(8,128)(2,1)S(1)}, bf16[256,1536]{1,0:T(8,128)(2,1)}, u32[]{:S(2)}) %copy-start.1) | copy-done | bytes 786456
  2.8 0.0 copy-start.2
  2.8 1.1 %copy-done.2 = bf16[256,1536]{1,0:T(8,128)(2,1)S(1)} copy-done((bf16[256,1536]{1,0:T(8,128)(2,1)S(1)}, bf16[256,1536]{1,0:T(8,128)(2,1)}, u32[]{:S(2)}) %copy-start.2) | copy-done | bytes 786456
  3.9 0.0 copy-start.3
  3.9 1.1 %copy-done.3 = bf16[1536,256]{1,0:T(8,128)(2,1)S(1)} copy-done((bf16[1536,256]{1,0:T(8,128)(2,1)S(1)}, bf16[1536,256]{1,0:T(8,128)(2,1)}, u32[]{:S(2)}) %copy-start.3) | copy-done | bytes 786456
  5.0 0.0 copy-start.4
  5.0 1.1 %copy-done.4 = bf16[1536,256]{1,0:T(8,128)(2,1)S(1)} copy-done((bf16[1536,256]{1,0:T(8,128)(2,1)S(1)}, bf16[1536,256]{1,0:T(8,128)(2,1)}, u32[]{:S(2)}) %copy-start.4) | copy-done | bytes 786456
  6.2 0.0 copy-start.5
  6.2 0.9 %copy-done.5 = f32[2,2,32,256]{3,2,1,0:T(8,128)S(1)} copy-done((f32[2,2,32,256]{3,2,1,0:T(8,128)S(1)}, f32[2,2,32,256]{3,2,1,0:T(8,128)}, u32[]{:S(2)}) %copy-start.5) | copy-done | bytes 131096
  7.1 0.0 copy-start.6
  7.1 0.8 %copy-done.6 = f32[128,128]{1,0:T(8,128)S(1)} copy-done((f32[128,128]{1,0:T(8,128)S(1)}, f32[128,128]{1,0:T(8,128)}, u32[]{:S(2)}) %copy-start.6) | copy-done | bytes 65560
  7.9 0.0 copy-start.7
  7.9 0.7 %copy-done.7 = f32[8,768]{1,0:T(8,128)S(1)} copy-done((f32[8,768]{1,0:T(8,128)S(1)}, f32[8,768]{1,0:T(8,128)}, u32[]{:S(2)}) %copy-start.7) | copy-done | bytes 24600
  8.6 53.6 %shard_map.82 = f32[32,17280]{1,0:T(8,128)S(1)} custom-call(f32[32,17280]{1,0:T(8,128)S(1)} %copy-done, f32[2,2,32,256]{3,2,1,0:T(8,128)S(1)} %copy-done.5, bf16[1536,256]{1,0:T(8,128)(2,1)S(1)} %copy-done.4, bf16[1536,256]{1,0:T(8,128)(2,1)S(1)} %copy-done.3, bf16[256,1536]{1,0:T(8,128)(2,1)S(1)} %copy-done.2, bf16[256,1536]{1,0:T(8,128)(2,1)S(1)} %copy-done.1, ...), custom_call_target="tpu_custom_call" | custom-call | flops 2000000000 | bytes 8000000 | tf_op jit(solution)/shard_map/pallas_call | solution.py:358
  62.3 1.4 %copy.10 = f32[32,17280]{1,0:T(8,128)} copy(f32[32,17280]{1,0:T(8,128)S(1)} %shard_map.82) | data formatting | bytes 4423680
Async XLA Ops:
  0.0 1.6 %copy-start = (f32[32,17280]{1,0:T(8,128)S(1)}, f32[32,17280]{1,0:T(8,128)}, u32[]{:S(2)}) copy-start(f32[32,17280]{1,0:T(8,128)} %x_hbm.1) | copy-start | bytes 6635524
  1.6 1.1 %copy-start.1 = (bf16[256,1536]{1,0:T(8,128)(2,1)S(1)}, bf16[256,1536]{1,0:T(8,128)(2,1)}, u32[]{:S(2)}) copy-start(bf16[256,1536]{1,0:T(8,128)(2,1)} %constant.15.clone.il_hbm) | copy-start | bytes 2359300
  2.8 1.1 %copy-start.2 = (bf16[256,1536]{1,0:T(8,128)(2,1)S(1)}, bf16[256,1536]{1,0:T(8,128)(2,1)}, u32[]{:S(2)}) copy-start(bf16[256,1536]{1,0:T(8,128)(2,1)} %constant.14.clone.ih_hbm) | copy-start | bytes 2359300
  3.9 1.1 %copy-start.3 = (bf16[1536,256]{1,0:T(8,128)(2,1)S(1)}, bf16[1536,256]{1,0:T(8,128)(2,1)}, u32[]{:S(2)}) copy-start(bf16[1536,256]{1,0:T(8,128)(2,1)} %constant.13.clone.fl_hbm) | copy-start | bytes 2359300
  5.0 1.1 %copy-start.4 = (bf16[1536,256]{1,0:T(8,128)(2,1)S(1)}, bf16[1536,256]{1,0:T(8,128)(2,1)}, u32[]{:S(2)}) copy-start(bf16[1536,256]{1,0:T(8,128)(2,1)} %constant.12.clone.fh_hbm) | copy-start | bytes 2359300
  6.2 0.9 %copy-start.5 = (f32[2,2,32,256]{3,2,1,0:T(8,128)S(1)}, f32[2,2,32,256]{3,2,1,0:T(8,128)}, u32[]{:S(2)}) copy-start(f32[2,2,32,256]{3,2,1,0:T(8,128)} %mix_hbm.1) | copy-start | bytes 393220
  7.1 0.8 %copy-start.6 = (f32[128,128]{1,0:T(8,128)S(1)}, f32[128,128]{1,0:T(8,128)}, u32[]{:S(2)}) copy-start(f32[128,128]{1,0:T(8,128)} %constant.17.clone.ldt) | copy-start | bytes 196612
  7.9 0.7 %copy-start.7 = (f32[8,768]{1,0:T(8,128)S(1)}, f32[8,768]{1,0:T(8,128)}, u32[]{:S(2)}) copy-start(f32[8,768]{1,0:T(8,128)} %constant.16.clone.rowc) | copy-start | bytes 73732

commit v2 on v1

--- a/solution.py
+++ b/solution.py
@@ -20,6 +20,8 @@
 GROUP = 4
 GROUPS = 3
 SPAN = GROUP * NLON
+PAIRS = NLAT // 2
+OWN = 6
 MESH = pl.DeviceIdType.MESH
 F32 = jnp.float32
 BF16 = jnp.bfloat16
@@ -47,8 +49,7 @@
 
 def row_constants():
     j = np.arange(NLAT)
-    place = j // 256, j % 256 // GROUP, j % GROUP
-    row = 12 * place[1] + GROUP * place[0] + place[2]
+    row = 2 * (j % PAIRS) + j // PAIRS
     theta = np.pi * (row + 0.5) / NLAT
     out = np.zeros((8, NLAT))
     out[0] = np.cos(theta)
@@ -83,35 +84,28 @@
     z = both[:128] + both[128:] + dot(high, fl)
     lt = lane_mask(32)
     out = []
-    for p in range(2):
+    for mh in range(2):
         pieces = []
-        for half in range(2):
-            z0 = z[64 * p : 64 * p + 32, 128 * half : 128 * half + 128]
-            z1 = z[64 * p + 32 : 64 * p + 64, 128 * half : 128 * half + 128]
+        for jj in range(2):
+            z0 = z[32 * jj : 32 * jj + 32, 128 * mh : 128 * mh + 128]
+            z1 = z[64 + 32 * jj : 96 + 32 * jj, 128 * mh : 128 * mh + 128]
             pieces.append(jnp.where(lt, z0, pltpu.roll(z1, 64, 1)))
             pieces.append(jnp.where(lt, pltpu.roll(z0, 64, 1), z1))
-        v = jnp.concatenate(pieces, 0).T
-        out += [v[:64], v[64:]]
+        out.append(jnp.concatenate(pieces, 0).T)
     return out
 
 
-def backward_lhs(quarters):
+def backward_lhs(v):
     lt = lane_mask(32)
-    rows = []
-    for p in range(2):
-        u = jnp.concatenate([quarters[2 * p], quarters[2 * p + 1]], 0).T
-        u0, u1, u2, u3 = (u[32 * q : 32 * q + 32] for q in range(4))
-        rows.append(
-            jnp.concatenate(
-                [jnp.where(lt, u0, pltpu.roll(u1, 64, 1)), jnp.where(lt, u2, pltpu.roll(u3, 64, 1))], 1
-            )
-        )
-        rows.append(
-            jnp.concatenate(
-                [jnp.where(lt, pltpu.roll(u0, 64, 1), u1), jnp.where(lt, pltpu.roll(u2, 64, 1), u3)], 1
-            )
-        )
-    return jnp.concatenate(rows, 0)
+    rows = [[], [], [], []]
+    for mh in range(2):
+        u = v[mh].T
+        for jj in range(2):
+            u0 = u[64 * jj : 64 * jj + 32]
+            u1 = u[64 * jj + 32 : 64 * jj + 64]
+            rows[jj].append(jnp.where(lt, u0, pltpu.roll(u1, 64, 1)))
+            rows[2 + jj].append(jnp.where(lt, pltpu.roll(u0, 64, 1), u1))
+    return jnp.concatenate([jnp.concatenate(r, 1) for r in rows], 0)
 
 
 def gelu(v):
@@ -158,39 +152,38 @@
         table[128 * mh + 120 : 128 * mh + 128, :] = jnp.zeros((8, NLAT), F32)
     lax.fori_loop(0, L, advance, (zero,) * 4)
 
-    def lay(g, _):
-        part = table[:, pl.ds(pl.multiple_of(256 * g, 256), 256)]
-        weight = rowc[2:3, pl.ds(pl.multiple_of(256 * g, 256), 256)]
-        high, low = halves(part * weight)
-        pw[0, g], pw[1, g] = high, low
-        high, low = halves(part.T)
-        pt[0, g], pt[1, g] = high, low
-        return 0
-
-    lax.fori_loop(0, GROUPS, lay, 0)
+    for mh in range(2):
+        for jj in range(2):
+            part = table[128 * mh : 128 * mh + 128, PAIRS * jj : PAIRS * jj + PAIRS]
+            high, low = halves(part * rowc[2:3, PAIRS * jj : PAIRS * jj + PAIRS])
+            at = slice(128 * jj, 128 * jj + 128)
+            pw[0, mh, at], pw[1, mh, at] = high, low
+            high, low = halves(part.T)
+            pt[0, mh, :, at], pt[1, mh, :, at] = high, low
 
 
 def mixing_tables(mixv, wm):
     group = lax.broadcasted_iota(jnp.int32, (32, 128), 1) // 32
-    for src in range(CHANS):
-        at, g = src // 4, src % 4
-        pieces = []
-        for mh in range(2):
+    for mh in range(2):
+        for src in range(CHANS):
+            at, g = src // 4, src % 4
             re = mixv[mh, 0][:, 128 * at : 128 * at + 128]
             im = mixv[mh, 1][:, 128 * at : 128 * at + 128]
-            for a, b in ((re, -im), (im, re)):
-                put = lambda v, to: jnp.where(
-                    group == to, v if to == g else pltpu.roll(v, 32 * ((to - g) % 4), 1), 0.0
-                )
-                pieces.append(put(a, 2 * mh) + put(b, 2 * mh + 1))
-        high, low = halves(jnp.concatenate(pieces, 0).T)
-        wm[128 * src : 128 * src + 128, :] = jnp.concatenate([high, low], 1)
+            pieces = []
+            for lh in range(2):
+                for a, b in ((re, -im), (im, re)):
+                    put = lambda v, to: jnp.where(
+                        group == to, v if to == g else pltpu.roll(v, 32 * ((to - g) % 4), 1), 0.0
+                    )
+                    pieces.append(put(a, 2 * lh) + put(b, 2 * lh + 1))
+            high, low = halves(jnp.concatenate(pieces, 0).T)
+            wm[mh, 128 * src : 128 * src + 128, :] = jnp.concatenate([high, low], 1)
 
 
 def kernel(
-    x_hbm, mix_hbm, fh_hbm, fl_hbm, ih_hbm, il_hbm, rowc, ldt, out_hbm,
-    xv, fv, iv, mixv, sent, got, back, home, gath, coef, table, pw, pt, wm, ybuf, yv,
-    xsem, fsem, isem, msem, osem, send1, recv1, send2, recv2, gsend, grecv,
+    x_hbm, mix_hbm, fh_hbm, fl_hbm, ih_hbm, il_hbm, rowc_hbm, ldt_hbm, out_hbm,
+    rowc, ldt, xv, fv, iv, mixv, sent, got, back, home, gath, coef, table, pw, pt, wm, ybuf, yv,
+    csem, xsem, fsem, isem, msem, osem, send1, recv1, send2, recv2, gsend, grecv,
 ):
     me = lax.axis_index("lat")
     ch = lax.axis_index("chan")
@@ -217,6 +210,12 @@
     for g in range(GROUPS):
         x_copy(g).start()
     m_copy.start()
+    c_copies = [
+        pltpu.make_async_copy(rowc_hbm, rowc, csem.at[0]),
+        pltpu.make_async_copy(ldt_hbm, ldt, csem.at[1]),
+    ]
+    c_copies[0].start()
+    c_copies[1].start()
     i_copies[0].start()
     i_copies[1].start()
 
@@ -238,29 +237,29 @@
     lax.fori_loop(1, CHANS, greet_chan, 0)
     pl.semaphore_wait(barrier, BANDS - 1 + CHANS - 1)
 
-    def spread(src, dst, send, recv, g):
+    def spread(src, dst, send, recv, mh):
         def one(i, _):
             peer = lax.rem(me + i, BANDS)
             pltpu.make_async_remote_copy(
-                src_ref=src.at[g, pl.ds(pl.multiple_of(4 * peer, 4), 4)],
-                dst_ref=dst.at[g, pl.ds(pl.multiple_of(4 * me, 4), 4)],
-                send_sem=send.at[g],
-                recv_sem=recv.at[g],
+                src_ref=src.at[mh, pl.ds(OWN * peer, OWN)],
+                dst_ref=dst.at[mh, pl.ds(OWN * me, OWN)],
+                send_sem=send.at[mh],
+                recv_sem=recv.at[mh],
                 device_id=(peer, ch),
                 device_id_type=MESH,
             ).start()
             return 0
 
         lax.fori_loop(1, BANDS, one, 0)
-        own = pl.ds(pl.multiple_of(4 * me, 4), 4)
-        pltpu.make_async_copy(src.at[g, own], dst.at[g, own], recv.at[g]).start()
-
-    def arrived(dst, recv, g):
-        pltpu.make_async_copy(dst.at[g], dst.at[g], recv.at[g]).wait()
-
-    def gone(src, send, g):
-        most = pl.ds(0, 4 * (BANDS - 1))
-        pltpu.make_async_copy(src.at[g, most], src.at[g, most], send.at[g]).wait()
+        own = pl.ds(OWN * me, OWN)
+        pltpu.make_async_copy(src.at[mh, own], dst.at[mh, own], recv.at[mh]).start()
+
+    def arrived(dst, recv, mh):
+        pltpu.make_async_copy(dst.at[mh], dst.at[mh], recv.at[mh]).wait()
+
+    def gone(src, send, mh):
+        most = pl.ds(0, OWN * (BANDS - 1))
+        pltpu.make_async_copy(src.at[mh, most], src.at[mh, most], send.at[mh]).wait()
 
     f_copies[0].wait()
     f_copies[1].wait()
@@ -268,57 +267,75 @@
     def dft(g, _):
         x_copy(g).wait()
         parts = forward_rows(xv[g], fv[0], fv[1])
-        for s in range(GROUP):
-            sent[g, pl.ds(s, BANDS, stride=GROUP), :] = parts[s]
-        spread(sent, got, send1, recv1, g)
+        for mh in range(2):
+            for p in range(2):
+                sent[mh, pl.ds(2 * g + p, BANDS, stride=OWN), :] = parts[mh][64 * p : 64 * p + 64]
         return 0
 
     lax.fori_loop(0, GROUPS, dft, 0)
-
+    for mh in range(2):
+        spread(sent, got, send1, recv1, mh)
+
+    c_copies[0].wait()
+    c_copies[1].wait()
     legendre_tables(me, rowc, ldt, coef, table, pw, pt)
     m_copy.wait()
     mixing_tables(mixv, wm)
 
-    total = jnp.zeros((256, 128), F32)
-    for g in range(GROUPS):
-        arrived(got, recv1, g)
-        high, low = halves(got[g])
-        both = dot(pw[0, g], jnp.concatenate([high, low], 1))
-        total = total + both[:, :128] + both[:, 128:] + dot(pw[1, g], high)
-    lt = lane_mask(128)
-    gath[ch] = jnp.where(lt, total[:128], total[128:])
-
-    def gather(i):
+    def gather(mh, i):
         return pltpu.make_async_remote_copy(
-            src_ref=gath.at[ch],
-            dst_ref=gath.at[ch],
-            send_sem=gsend.at[i],
-            recv_sem=grecv.at[i],
+            src_ref=gath.at[mh, ch],
+            dst_ref=gath.at[mh, ch],
+            send_sem=gsend.at[mh, i],
+            recv_sem=grecv.at[mh, i],
             device_id=(me, lax.rem(ch + i, CHANS)),
             device_id_type=MESH,
         )
 
-    for i in range(1, CHANS):
-        gather(i).start()
-    for i in range(1, CHANS):
-        gather(i).wait()
-    high, low = halves(jnp.concatenate([gath[src] for src in range(CHANS)], 1))
-    both = dot(high, wm[...])
-    mixed = both[:, :128] + both[:, 128:] + dot(low, wm[:, :128])
-
-    stacked = jnp.concatenate([jnp.where(lt, mixed, 0.0), jnp.where(lt, 0.0, mixed)], 0)
-    mhigh, mlow = halves(stacked)
-    mboth = jnp.concatenate([mhigh, mlow], 1)
-    for g in range(GROUPS):
-        both = dot(pt[0, g], mboth)
-        back[g] = both[:, :128] + both[:, 128:] + dot(pt[1, g], mhigh)
-        spread(back, home, send2, recv2, g)
+    lt = lane_mask(128)
+    lt64 = lane_mask(64)
+    for mh in range(2):
+        arrived(got, recv1, mh)
+        high, low = halves(got[mh])
+        both = dot(pw[0, mh], jnp.concatenate([high, low], 1))
+        total = both[:, :128] + both[:, 128:] + dot(pw[1, mh], high)
+        both = jnp.where(lt, total[:128], total[128:])
+        both = both + pltpu.roll(both, 64, 1)
+        gath[mh, ch] = jnp.where(lt64, both[:64], both[64:])
+        for i in range(1, CHANS):
+            gather(mh, i).start()
+
+    for mh in range(2):
+        for i in range(1, CHANS):
+            gather(mh, i).wait()
+        high, low = halves(jnp.concatenate([gath[mh, src] for src in range(CHANS)], 1))
+        both = dot(high, wm[mh])
+        mixed = both[:, :128] + both[:, 128:] + dot(low, wm[mh, :, :128])
+        turned = pltpu.roll(mixed, 64, 1)
+        stacked = jnp.concatenate(
+            [
+                jnp.where(lt64, mixed, 0.0),
+                jnp.where(lt64, turned, 0.0),
+                jnp.where(lt64, 0.0, turned),
+                jnp.where(lt64, 0.0, mixed),
+            ],
+            0,
+        )
+        mhigh, mlow = halves(stacked)
+        both = dot(pt[0, mh], jnp.concatenate([mhigh, mlow], 1))
+        back[mh] = both[:, :128] + both[:, 128:] + dot(pt[1, mh], mhigh)
+        spread(back, home, send2, recv2, mh)
     i_copies[0].wait()
     i_copies[1].wait()
+    for mh in range(2):
+        arrived(home, recv2, mh)
 
     def inverse(g, _):
-        arrived(home, recv2, g)
-        z = backward_lhs([home[g, pl.ds(s, BANDS, stride=GROUP), :] for s in range(GROUP)])
+        v = [
+            jnp.concatenate([home[mh, pl.ds(2 * g + p, BANDS, stride=OWN), :] for p in range(2)], 0)
+            for mh in range(2)
+        ]
+        z = backward_lhs(v)
         high, low = halves(z)
         stack = jnp.concatenate([high, low], 0)
         for t in range(WIN // 256):
@@ -343,24 +360,26 @@
 
     lax.fori_loop(0, GROUPS, inverse, 0)
     for g in range(GROUPS):
-        gone(sent, send1, g)
-        gone(back, send2, g)
         out_copy(g).wait()
+    for mh in range(2):
+        gone(sent, send1, mh)
+        gone(back, send2, mh)
 
 
 def shards(field, mixing):
     (fh, fl), (ih, il) = dft_tables()
     rowc, ldt = row_constants()
-    anywhere = pl.BlockSpec(memory_space=pl.ANY)
-    inside = pl.BlockSpec(memory_space=pltpu.VMEM)
+    anywhere = pl.BlockSpec(memory_space=pltpu.HBM)
     dma = pltpu.SemaphoreType.DMA
-    exchange = pltpu.VMEM((GROUPS, 4 * BANDS, 128), F32)
+    exchange = pltpu.VMEM((2, PAIRS, 128), F32)
     return pl.pallas_call(
         kernel,
         out_shape=jax.ShapeDtypeStruct(field.shape, F32),
-        in_specs=[anywhere] * 6 + [inside] * 2,
+        in_specs=[anywhere] * 8,
         out_specs=anywhere,
         scratch_shapes=[
+            pltpu.VMEM((8, NLAT), F32),
+            pltpu.VMEM((MODES, 128), F32),
             pltpu.VMEM((GROUPS, 32, SPAN), F32),
             pltpu.VMEM((2, WIN, 256), BF16),
             pltpu.VMEM((2, 256, WIN), BF16),
@@ -369,28 +388,29 @@
             exchange,
             exchange,
             exchange,
-            pltpu.VMEM((CHANS, 128, 128), F32),
+            pltpu.VMEM((2, CHANS, 64, 128), F32),
             pltpu.VMEM((6, 128, 128), F32),
             pltpu.VMEM((256, NLAT), F32),
-            pltpu.VMEM((2, GROUPS, 256, 256), BF16),
-            pltpu.VMEM((2, GROUPS, 256, 256), BF16),
-            pltpu.VMEM((128 * CHANS, 256), BF16),
+            pltpu.VMEM((2, 2, 256, PAIRS), BF16),
+            pltpu.VMEM((2, 2, PAIRS, 256), BF16),
+            pltpu.VMEM((2, 128 * CHANS, 256), BF16),
             pltpu.VMEM((128, WIN), F32),
             pltpu.VMEM((GROUPS, 32, SPAN), F32),
+            dma((2,)),
             dma((GROUPS,)),
             dma((2,)),
             dma((2,)),
             dma,
             dma((GROUPS,)),
-            dma((GROUPS,)),
-            dma((GROUPS,)),
-            dma((GROUPS,)),
-            dma((GROUPS,)),
-            dma((CHANS,)),
-            dma((CHANS,)),
+            dma((2,)),
+            dma((2,)),
+            dma((2,)),
+            dma((2,)),
+            dma((2, CHANS)),
+            dma((2, CHANS)),
         ],
         compiler_params=pltpu.CompilerParams(
-            collective_id=0, has_side_effects=True, vmem_limit_bytes=40 << 20
+            collective_id=0, has_side_effects=True, vmem_limit_bytes=60 << 20
         ),
         cost_estimate=pl.CostEstimate(flops=2_000_000_000, bytes_accessed=8_000_000, transcendentals=600_000),
     )(

time: 64.1 us -> 55.9 us (0.87)
  local copies, waits for them, and re-layouts: 9.99 us -> 3.12 us
  Pallas kernels: 53.6 us -> 52.6 us
    unnamed x17 -> x1, local copies, waits for them, and re-layouts: 9.99 us -> 3.12 us
    pallas_call x1, Pallas kernels: 53.6 us -> 52.6 us  [shards(): pl.pallas_call(kernel, out_shape=jax.ShapeDtypeStruct(field.shape, F32),...]
where the time goes in v2:
time: 55.9 us; the launch traced here: 55.7 us
  Pallas kernels  52.6 us (94%)
  local copies, waits for them, and re-layouts  3.12 us (6%)
    pallas_call x1, Pallas kernels, shards(): pl.pallas_call(kernel, out_shape=jax.ShapeDtypeStruct(field.shape, F32),...  52.6 us
    unnamed x1, local copies, waits for them, and re-layouts  3.12 us

profile of v2, /device:TPU:1, one launch (start us, length us, event | category | flops | bytes accessed | tf_op | source)
XLA Modules:
  0.0 55.7 jit_solution(1497079007362133394)
XLA Ops:
  0.0 52.6 %shard_map.82 = f32[32,17280]{1,0:T(8,128)} custom-call(f32[32,17280]{1,0:T(8,128)} %x_hbm.1, f32[2,2,32,256]{3,2,1,0:T(8,128)} %mix_hbm.1, bf16[1536,256]{1,0:T(8,128)(2,1)} %constant.12.clone.fh_hbm, bf16[1536,256]{1,0:T(8,128)(2,1)} %constant.13.clone.fl_hbm, bf16[256,1536]{1,0:T(8,128)(2,1)} %constant.14.clone.ih_hbm, ...), custom_call_target="tpu_custom_call" | custom-call | flops 2000000000 | bytes 8000000 | tf_op jit(solution)/shard_map/pallas_call | solution.py:375
  52.6 3.1 %copy.10 = f32[32,17280]{1,0:T(8,128)} copy(f32[32,17280]{1,0:T(8,128)} %shard_map.82) | data formatting | bytes 4423680

commit v3 on v2

--- a/solution.py
+++ b/solution.py
@@ -187,6 +187,27 @@
 ):
     me = lax.axis_index("lat")
     ch = lax.axis_index("chan")
+
+    barrier = pltpu.get_barrier_semaphore()
+
+    def far_first(i):
+        turn = lambda r: jnp.where(lax.rem(r, 2) == 1, 4 - (r + 1) // 2, 4 + r // 2)
+        z = lax.rem(me // 8 + turn(i // 8), 8)
+        y = lax.rem(lax.rem(me, 8) + turn(lax.rem(i, 8)), 8)
+        return z * 8 + y
+
+    def greet_lat(i, _):
+        pl.semaphore_signal(barrier, inc=1, device_id=(far_first(i), ch), device_id_type=MESH)
+        return 0
+
+    def greet_chan(i, _):
+        pl.semaphore_signal(
+            barrier, inc=1, device_id=(me, lax.rem(ch + i, CHANS)), device_id_type=MESH
+        )
+        return 0
+
+    lax.fori_loop(0, BANDS - 1, greet_lat, 0)
+    lax.fori_loop(1, CHANS, greet_chan, 0)
 
     def x_copy(g):
         return pltpu.make_async_copy(
@@ -219,27 +240,10 @@
     i_copies[0].start()
     i_copies[1].start()
 
-    barrier = pltpu.get_barrier_semaphore()
-
-    def greet_lat(i, _):
-        pl.semaphore_signal(
-            barrier, inc=1, device_id=(lax.rem(me + i, BANDS), ch), device_id_type=MESH
-        )
-        return 0
-
-    def greet_chan(i, _):
-        pl.semaphore_signal(
-            barrier, inc=1, device_id=(me, lax.rem(ch + i, CHANS)), device_id_type=MESH
-        )
-        return 0
-
-    lax.fori_loop(1, BANDS, greet_lat, 0)
-    lax.fori_loop(1, CHANS, greet_chan, 0)
-    pl.semaphore_wait(barrier, BANDS - 1 + CHANS - 1)
 
     def spread(src, dst, send, recv, mh):
         def one(i, _):
-            peer = lax.rem(me + i, BANDS)
+            peer = far_first(i)
             pltpu.make_async_remote_copy(
                 src_ref=src.at[mh, pl.ds(OWN * peer, OWN)],
                 dst_ref=dst.at[mh, pl.ds(OWN * me, OWN)],
@@ -250,7 +254,7 @@
             ).start()
             return 0
 
-        lax.fori_loop(1, BANDS, one, 0)
+        lax.fori_loop(0, BANDS - 1, one, 0)
         own = pl.ds(OWN * me, OWN)
         pltpu.make_async_copy(src.at[mh, own], dst.at[mh, own], recv.at[mh]).start()
 
@@ -273,6 +277,7 @@
         return 0
 
     lax.fori_loop(0, GROUPS, dft, 0)
+    pl.semaphore_wait(barrier, BANDS - 1 + CHANS - 1)
     for mh in range(2):
         spread(sent, got, send1, recv1, mh)
 
@@ -307,7 +312,7 @@
 
     for mh in range(2):
         for i in range(1, CHANS):
-            gather(mh, i).wait()
+            gather(mh, i).wait_recv()
         high, low = halves(jnp.concatenate([gath[mh, src] for src in range(CHANS)], 1))
         both = dot(high, wm[mh])
         mixed = both[:, :128] + both[:, 128:] + dot(low, wm[mh, :, :128])
@@ -364,6 +369,8 @@
     for mh in range(2):
         gone(sent, send1, mh)
         gone(back, send2, mh)
+        for i in range(1, CHANS):
+            gather(mh, i).wait_send()
 
 
 def shards(field, mixing):

time: 55.9 us -> 55.7 us (level)
  no operation moved by 1% of the time
where the time goes in v3:
time: 55.7 us; the launch traced here: 55.6 us
  Pallas kernels  52.5 us (94%)
  local copies, waits for them, and re-layouts  3.12 us (6%)
    pallas_call x1, Pallas kernels, shards(): pl.pallas_call(kernel, out_shape=jax.ShapeDtypeStruct(field.shape, F32),...  52.5 us
    unnamed x1, local copies, waits for them, and re-layouts  3.12 us

profile of v3, /device:TPU:1, one launch (start us, length us, event | category | flops | bytes accessed | tf_op | source)
XLA Modules:
  0.0 55.6 jit_solution(2888556738618597681)
XLA Ops:
  0.0 52.5 %shard_map.82 = f32[32,17280]{1,0:T(8,128)} custom-call(f32[32,17280]{1,0:T(8,128)} %x_hbm.1, f32[2,2,32,256]{3,2,1,0:T(8,128)} %mix_hbm.1, bf16[1536,256]{1,0:T(8,128)(2,1)} %constant.12.clone.fh_hbm, bf16[1536,256]{1,0:T(8,128)(2,1)} %constant.13.clone.fl_hbm, bf16[256,1536]{1,0:T(8,128)(2,1)} %constant.14.clone.ih_hbm, ...), custom_call_target="tpu_custom_call" | custom-call | flops 2000000000 | bytes 8000000 | tf_op jit(solution)/shard_map/pallas_call | solution.py:382
  52.5 3.1 %copy.10 = f32[32,17280]{1,0:T(8,128)} copy(f32[32,17280]{1,0:T(8,128)} %shard_map.82) | data formatting | bytes 4423680
